TPU v7x, 1024 devices: a whole 4x4x32 slice. The times are simulated.
1024 devices in a mesh: dp: 64 (over z, core), tensor: 16 (over x, y).
Axes of the slice: x: 4, y: 4, z: 32, core: 2. Of those that a mesh axis runs over, the one named last changes fastest.
Arguments:
- activations: bfloat16 [49152, 4096], P('dp', 'tensor'), may hold values from -0.21875 to 0.21875
- out_grads: bfloat16 [49152, 4096], P('dp'), may hold values from -6 to 6
- error_memory: bfloat16 [64, 4096, 4096], P('dp', 'tensor'), may hold values from -6 to 6
- q_init: float32 [4096, 64], replicated, may hold values from -0.09375 to 0.09375
Outputs:
- p_basis: float32 [4096, 64], P('tensor')
- q_factor: float32 [4096, 64], replicated
All inputs are finite; a program needn't handle non-finite values.
Results may differ from a plain program's by a relative error of at most 0.0003.
Values sent between devices are 32-bit elements; how exact they have to be, the bound alone decides.
A program may use at most 64 MiB of HBM per device.

v0:
```python
import jax
import jax.numpy as jnp
from jax import lax
from jax.sharding import PartitionSpec as P


def local(activations, out_grads, error_memory, q_init):
    highest = lax.Precision.HIGHEST
    memory = error_memory[0].astype(jnp.float32)
    contract_rows = (((0,), (0,)), ((), ()))
    corrected = (
        lax.dot_general(activations, out_grads, contract_rows, preferred_element_type=jnp.float32)
        + memory
    )
    p_local = jnp.dot(corrected, q_init, precision=highest)
    p_sum = lax.psum(p_local, "dp")
    whole_left = lax.all_gather(p_sum, "tensor", axis=0, tiled=True)
    gram = jnp.dot(whole_left.T, whole_left, precision=highest)
    lower = jnp.linalg.cholesky(gram)
    p_orth = lax.linalg.triangular_solve(
        lower, p_sum, left_side=False, lower=True, transpose_a=True
    )
    q_local = lax.dot_general(
        corrected, p_orth, contract_rows, precision=highest, preferred_element_type=jnp.float32
    )
    replicas = lax.axis_size("dp")
    q_total = lax.psum(q_local, ("dp", "tensor"))
    total_rows = p_orth.shape[0] * lax.axis_size("tensor")
    return (p_orth * jnp.sqrt(jnp.float32(total_rows)), q_total / replicas)


def solution(mesh):
    return jax.shard_map(
        local,
        mesh=mesh,
        in_specs=(P("dp", "tensor"), P("dp", None), P("dp", "tensor", None), P()),
        out_specs=(P("tensor", None), P()),
        check_vma=False,
    )
```

profile of v0, /device:TPU:1, one launch (start us, length us, event | category | flops | bytes accessed | tf_op | source)
XLA Modules:
  0.0 1371.7 jit_solution(16299675796303356587)
XLA Ops:
  7.2 0.0 copy-start
  7.2 0.0 all-reduce.3.cloned.1.call-start
  7.2 5.5 convolution_add_fusion
  12.8 0.0 copy-start.1
  12.8 1.9 copy-done.1
  14.7 0.0 copy-done
  14.7 4.6 fusion.4
  19.3 0.0 all-reduce.3.cloned.1.call-update
  19.3 0.0 all-gather.2.cloned.1.call-start
  19.4 363.6 %all-reduce.3.cloned.1.call-done = f32[256,64]{0,1:T(8,128)} async-done(((f32[256,64]{0,1:T(8,128)}), f32[256,64]{0,1:T(8,128)}) %all-reduce.3.cloned.1.call-update) | async-done | bytes 65552 | tf_op jit(solution)/shard_map/psum | solution.py:16
  382.9 0.0 all-gather.2.cloned.1.call-update
  382.9 0.0 all-reduce.5.cloned.1.call-start
  383.0 64.6 %all-gather.2.cloned.1.call-done = f32[4096,64]{0,1:T(8,128)} async-done(((f32[256,64]{0,1:T(8,128)}), f32[4096,64]{0,1:T(8,128)}) %all-gather.2.cloned.1.call-update) | async-done | bytes 1048592 | tf_op jit(solution)/shard_map/all_gather | solution.py:17
  447.6 2.5 fusion.5
  450.1 0.1 copy.6
  450.2 5.8 cholesky.16
  456.1 0.6 compare_reduce_fusion
  456.7 0.7 fusion
  457.4 4.9 custom-call.6
  462.3 1.7 broadcast_multiply_fusion.1
  464.0 6.0 fusion.6
  470.0 0.0 all-reduce.5.cloned.1.call-update
  470.0 892.9 %all-reduce.5.cloned.1.call-done = f32[4096,64]{0,1:T(8,128)} async-done(((f32[4096,64]{0,1:T(8,128)}), f32[4096,64]{0,1:T(8,128)}) %all-reduce.5.cloned.1.call-update) | async-done | bytes 1048592 | tf_op jit(solution)/shard_map/psum | solution.py:27
  1362.9 2.3 broadcast_multiply_fusion
  (2 shorter events, 0.0 us)
Async XLA Ops:
  7.2 7.6 copy-start
  7.2 375.7 %all-reduce.3.cloned.1.call-start = ((), (), s32[]{:S(2)}) async-start(), calls=%async_computation | async-start | bytes 131072 | tf_op jit(solution)/shard_map/psum | solution.py:16
  12.8 1.9 copy-start.1
  19.3 428.3 %all-gather.2.cloned.1.call-start = ((), (), s32[]{:S(2)}) async-start(), calls=%async_computation.1 | async-start | bytes 1114112 | tf_op jit(solution)/shard_map/all_gather | solution.py:17
  382.9 979.9 %all-reduce.5.cloned.1.call-start = ((), (), s32[]{:S(2)}) async-start(), calls=%async_computation.2 | async-start | bytes 2097152 | tf_op jit(solution)/shard_map/psum | solution.py:27
Sparse Core Ops, SparseCore 0:
  19.4 363.4 all-reduce.2
  387.8 59.7 all-gather.1
  470.1 892.7 all-reduce.4
where the time goes:
time: 1370 us
  waiting for transfers between devices  1320 us (96%)
  matrix products  20.3 us (1%)
  other arithmetic  14.3 us (1%)
  between operations  13.8 us (1%)
    psum x1, waiting for transfers between devices, local(): q_total = lax.psum(q_local, ('dp', 'tensor'))  893 us
    psum x1, waiting for transfers between devices, local(): p_sum = lax.psum(p_local, 'dp')  364 us
    all_gather x1, waiting for transfers between devices, local(): whole_left = lax.all_gather(p_sum, 'tensor', axis=0, tiled=True)  64.6 us
  transfers between devices with their start and end apart: 3, of which 3 were waited for; matrix products, arithmetic and copies ran while one was open for 0% of the time, Pallas kernels for 0%

commit v1 on v0

v1 whole, which is shorter than its diff:
```python
import jax
import jax.numpy as jnp
from jax import lax
from jax.experimental import pallas as pl
from jax.experimental.pallas import tpu as pltpu
from jax.sharding import PartitionSpec as P

MESH = pl.DeviceIdType.MESH
F32 = jnp.float32
BF16 = jnp.bfloat16
HIGHEST = lax.Precision.HIGHEST
NZ = 32
NT = 16
RANK = 64
LANES = 128
WIN = 8
GROUPS = NZ // WIN
LEFT, RIGHT = -(WIN // 2 - 1), WIN // 2
NN = (((1,), (0,)), ((), ()))
NT_DIMS = (((1,), (1,)), ((), ()))


def dot(a, b, dims=NN, precision=None):
    return lax.dot_general(a, b, dims, precision=precision, preferred_element_type=F32)


def split3(v):
    hi = v.astype(BF16)
    rest = v - hi.astype(F32)
    mid = rest.astype(BF16)
    low = (rest - mid.astype(F32)).astype(BF16)
    return jnp.concatenate([hi, mid, low], axis=0)


def fold3(v):
    return v[:RANK] + (v[RANK:2 * RANK] + v[2 * RANK:])


def wait(sem, ref):
    pltpu.make_async_copy(ref, ref, sem).wait()


def invert_factor(gram):
    row = lax.broadcasted_iota(jnp.int32, (RANK, 2 * RANK), 0)
    lane = lax.broadcasted_iota(jnp.int32, (RANK, 2 * RANK), 1)
    m = jnp.where(lane < RANK, gram, jnp.where(lane - RANK == row, 1.0, 0.0))
    scale = jnp.zeros((RANK, 2 * RANK), F32)
    for k in range(RANK):
        col = jnp.broadcast_to(m[:, k:k + 1], m.shape)
        pivot = col[k:k + 1, :]
        scaled = m[k:k + 1, :] / pivot
        scale = jnp.where(row == k, pivot, scale)
        m = m - jnp.where(row > k, col, 0.0) * scaled
    m = m * lax.rsqrt(scale)
    return m[:, RANK:]


def kernel(act_hbm, grd_hbm, err_hbm, q0_hbm, pb_ref, out_ref,
           x, act, q0, q3, w3, p_src, p_rs, p_far, p_red, p_all,
           g_src, g_rs, g_own, g_all,
           q_loc, q_d, q_s, q_x, z_src, z_rs, z_far, z_red, z_all,
           load_sem, send_sem, recv_sem, piece_sem):
    dp = lax.axis_index("dp")
    t = lax.axis_index("tensor")
    z = dp // 2
    core = dp % 2
    other = 1 - core
    place = z % WIN
    group = z // WIN

    def at(zz, cc):
        return ((zz + NZ) % NZ) * 2 + cc

    def send(src, dst, phase, dev, recv=None):
        pltpu.make_async_remote_copy(
            src_ref=src, dst_ref=dst, send_sem=send_sem.at[phase],
            recv_sem=recv_sem.at[phase] if recv is None else recv,
            device_id=dev, device_id_type=MESH).start()

    def tile(i):
        return pl.ds(pl.multiple_of(i * 8, 8), 8)

    copies = [pltpu.make_async_copy(q0_hbm, q0, load_sem.at[0])]
    copies.append(pltpu.make_async_copy(err_hbm, x.at[pl.ds(768, 256)], load_sem.at[1]))
    for r in range(3):
        copies.append(pltpu.make_async_copy(
            grd_hbm.at[pl.ds(256 * r, 256)], x.at[pl.ds(256 * r, 256)], load_sem.at[2 + r]))
    copies.append(pltpu.make_async_copy(act_hbm, act, load_sem.at[5]))
    for c in copies:
        c.start()

    barrier = pltpu.get_barrier_semaphore()
    near = [(d, c) for d in range(-WIN // 2, WIN // 2 + 1) for c in (0, 1)]
    for d, c in near:
        cc = core if c == 0 else other
        if (d, c) != (0, 0):
            pl.semaphore_signal(barrier, inc=1, device_id=(at(z + d, cc), t), device_id_type=MESH)
    for d in (-WIN, WIN):
        pl.semaphore_signal(barrier, inc=1, device_id=(at(z + d, core), t), device_id_type=MESH)
    for k in range(1, NT):
        pl.semaphore_signal(barrier, inc=1, device_id=(dp, t ^ k), device_id_type=MESH)

    copies[0].wait()
    q3[...] = split3(q0[...])
    copies[1].wait()
    left = fold3(dot(q3[...], x[768:1024, :], NT_DIMS))
    copies[5].wait()
    acc = None
    for r in range(3):
        copies[2 + r].wait()
        y = fold3(dot(q3[...], x[256 * r:256 * (r + 1), :], NT_DIMS))
        term = dot(split3(y), act[256 * r:256 * (r + 1), :])
        acc = term if acc is None else acc + term
    p_src[...] = fold3(acc) + left
    pl.semaphore_wait(barrier, 2 * (WIN + 1) - 1 + 2 + NT - 1)

    slot = 0
    for d in range(LEFT, RIGHT + 1):
        e = -d
        for same in (0, 1):
            if d == 0 and same == 1:
                continue
            cc = core if same else other
            piece = (z + e + NZ) % WIN
            send(p_src.at[tile(piece), pl.ds(pl.multiple_of(cc * LANES, LANES), LANES)],
                 p_rs.at[slot], 0, (at(z + e, cc), t))
            slot += 1
    own = p_src[tile(place), pl.ds(pl.multiple_of(core * LANES, LANES), LANES)]
    wait(recv_sem.at[0], p_rs)
    total = own
    for s in range(2 * WIN - 1):
        total = total + p_rs[s]
    p_far[group] = total
    send(p_far.at[group], p_far.at[group], 1, (at(z - WIN, core), t))
    send(p_far.at[group], p_far.at[group], 1, (at(z + WIN, core), t))
    wait(recv_sem.at[1], p_rs.at[pl.ds(0, 2)])
    step = 1 - 2 * core
    relay = (group + step + GROUPS) % GROUPS
    send(p_far.at[relay], p_far.at[relay], 2, (at(z - step * WIN, core), t))
    wait(recv_sem.at[2], p_rs.at[0])
    total = (p_far[0] + p_far[1]) + (p_far[2] + p_far[3])
    p_red[...] = total
    rows, cols = tile(place), pl.ds(pl.multiple_of(core * LANES, LANES), LANES)
    p_all[rows, cols] = total
    for d in range(LEFT, RIGHT + 1):
        for same in (0, 1):
            if d == 0 and same == 1:
                continue
            send(p_red, p_all.at[rows, cols], 3, (at(z + d, core if same else other), t))
    wait(recv_sem.at[3], p_rs)

    p_sum = p_all[...]
    gram = dot(p_sum, jnp.concatenate([p_sum, p_sum], axis=0), NT_DIMS, HIGHEST)
    for i in range(NT):
        g_src[i, 0:4, :] = gram[4 * i:4 * i + 4]
        g_src[i, 4:8, :] = gram[4 * i:4 * i + 4]
    for k in range(1, NT):
        send(g_src.at[t ^ k], g_rs.at[k - 1], 4, (dp, t ^ k))

    p3 = split3(p_sum)
    w3[:, 768:1024] = p3
    w3[:, 0:768] = split3(fold3(dot(p3, act[...], NT_DIMS)))

    def chunk(k):
        j = t ^ k
        v = fold3(dot(w3[...], x[:, pl.ds(pl.multiple_of(j * 256, 256), 256)]))
        q_loc[k, 0] = v[:, :LANES]
        q_loc[k, 1] = v[:, LANES:]
        send(q_loc.at[k, other], q_d.at[k], 5, (dp + other - core, t), piece_sem.at[k])

    def forward(k):
        wait(piece_sem.at[k], q_d.at[k])
        q_s[k] = q_loc[k, core] + q_d[k]
        if k > 0:
            send(q_s.at[k], q_x.at[k - 1], 6, (dp, t ^ k))

    order = list(range(1, NT)) + [0]
    lag = 6
    for i in range(NT + lag):
        if i < NT:
            chunk(order[i])
        if i >= lag:
            forward(order[i - lag])

    wait(recv_sem.at[4], g_rs)
    total = g_src[t]
    for k in range(NT - 1):
        total = total + g_rs[k]
    g_own[...] = total
    g_all[t] = total
    for k in range(1, NT):
        send(g_own, g_all.at[t], 7, (dp, t ^ k))

    wait(recv_sem.at[6], q_x)
    total = q_s[0]
    for k in range(NT - 1):
        total = total + q_x[k]
    z_src[...] = total

    slot = 0
    for d in range(LEFT, RIGHT + 1):
        if d != 0:
            piece = (z - d + NZ) % WIN
            send(z_src.at[tile(piece)], z_rs.at[slot], 8, (at(z - d, core), t))
            slot += 1
    own = z_src[tile(place)]
    wait(recv_sem.at[8], z_rs)
    total = own
    for s in range(WIN - 1):
        total = total + z_rs[s]
    z_far[group] = total
    for m in range(1, GROUPS):
        send(z_far.at[group], z_far.at[group], 9, (at(z + m * WIN, core), t))

    wait(recv_sem.at[7], g_rs)
    inverse = invert_factor(jnp.concatenate([g_all[i, 0:4, :] for i in range(NT)], axis=0))
    pb_ref[...] = dot(inverse, p_sum, NN, HIGHEST) * 64.0

    wait(recv_sem.at[9], z_rs.at[pl.ds(0, GROUPS - 1)])
    total = (z_far[0] + z_far[1]) + (z_far[2] + z_far[3])
    z_red[...] = total
    z_all[rows, :] = total
    for d in range(LEFT, RIGHT + 1):
        if d != 0:
            send(z_red, z_all.at[rows], 10, (at(z + d, core), t))
    wait(recv_sem.at[10], z_rs)

    def columns(tt, cc):
        return pl.ds(pl.multiple_of((tt * 2 + cc) * LANES, LANES), LANES)

    mine = columns(t, core)
    out_ref[:, mine] = dot(inverse, z_all[...], NN, HIGHEST) * (1.0 / 64.0)
    for k in range(1, NT):
        send(out_ref.at[:, mine], out_ref.at[:, mine], 11, (dp, t ^ k), piece_sem.at[NT + k])
    sibling = (dp + other - core, t)
    send(out_ref.at[:, mine], out_ref.at[:, mine], 12, sibling)
    for k in range(1, NT):
        got = columns(t ^ k, core)
        wait(piece_sem.at[NT + k], out_ref.at[:, got])
        send(out_ref.at[:, got], out_ref.at[:, got], 12, sibling)
    wait(recv_sem.at[12], q_d)

    wait(send_sem.at[0], p_rs)
    wait(send_sem.at[1], p_rs.at[pl.ds(0, 2)])
    wait(send_sem.at[2], p_rs.at[0])
    wait(send_sem.at[3], p_rs)
    wait(send_sem.at[4], g_rs)
    wait(send_sem.at[5], q_d)
    wait(send_sem.at[6], q_x)
    wait(send_sem.at[7], g_rs)
    wait(send_sem.at[8], z_rs)
    wait(send_sem.at[9], z_rs.at[pl.ds(0, GROUPS - 1)])
    wait(send_sem.at[10], z_rs)
    wait(send_sem.at[11], q_x)
    wait(send_sem.at[12], q_d)


def local(activations, out_grads, error_memory, q_init):
    any_spec = pl.BlockSpec(memory_space=pl.ANY)
    vmem = pl.BlockSpec(memory_space=pltpu.VMEM)
    piece = (RANK, LANES)
    scratch = [
        pltpu.VMEM((1024, 4096), BF16),
        pltpu.VMEM((768, 256), BF16),
        pltpu.VMEM((RANK, 4096), F32),
        pltpu.VMEM((3 * RANK, 4096), BF16),
        pltpu.VMEM((3 * RANK, 1024), BF16),
        pltpu.VMEM((RANK, 256), F32),
        pltpu.VMEM((2 * WIN - 1, 8, LANES), F32),
        pltpu.VMEM((GROUPS, 8, LANES), F32),
        pltpu.VMEM((8, LANES), F32),
        pltpu.VMEM((RANK, 256), F32),
        pltpu.VMEM((NT, 8, LANES), F32),
        pltpu.VMEM((NT - 1, 8, LANES), F32),
        pltpu.VMEM((8, LANES), F32),
        pltpu.VMEM((NT, 8, LANES), F32),
        pltpu.VMEM((NT, 2) + piece, F32),
        pltpu.VMEM((NT,) + piece, F32),
        pltpu.VMEM((NT,) + piece, F32),
        pltpu.VMEM((NT - 1,) + piece, F32),
        pltpu.VMEM(piece, F32),
        pltpu.VMEM((WIN - 1, 8, LANES), F32),
        pltpu.VMEM((GROUPS, 8, LANES), F32),
        pltpu.VMEM((8, LANES), F32),
        pltpu.VMEM(piece, F32),
        pltpu.SemaphoreType.DMA((6,)),
        pltpu.SemaphoreType.DMA((13,)),
        pltpu.SemaphoreType.DMA((13,)),
        pltpu.SemaphoreType.DMA((2 * NT,)),
    ]
    basis, right = pl.pallas_call(
        kernel,
        name="powersgd",
        out_shape=(
            jax.ShapeDtypeStruct((RANK, 256), F32),
            jax.ShapeDtypeStruct((RANK, 4096), F32),
        ),
        in_specs=[any_spec] * 4,
        out_specs=(vmem, vmem),
        scratch_shapes=scratch,
        compiler_params=pltpu.CompilerParams(
            collective_id=0, has_side_effects=True, vmem_limit_bytes=60 * 2**20),
    )(activations, out_grads, error_memory[0], q_init.T)
    return basis.T, right.T


def solution(mesh):
    return jax.shard_map(
        local,
        mesh=mesh,
        in_specs=(P("dp", "tensor"), P("dp", None), P("dp", "tensor", None), P()),
        out_specs=(P("tensor", None), P()),
        check_vma=False,
    )
```

time: 1370 us -> 103 us (0.08)
  waiting for transfers between devices: 1320 us -> 0 us
  Pallas kernels: 0 us -> 98.8 us
  matrix products: 20.3 us -> 0 us
  other arithmetic: 14.3 us -> 0 us
    psum x2 -> x0, waiting for transfers between devices: 1260 us -> none  [the longest x1 893 us: local(): q_total = lax.psum(q_local, ('dp', 'tensor'))]
    pallas_call x0 -> x1, Pallas kernels: none -> 98.8 us  [local(): pl.pallas_call(kernel, name='powersgd', out_shape=(jax.ShapeDtypeStruct((...]
    all_gather x1 -> x0, waiting for transfers between devices: 64.6 us -> none  [local(): whole_left = lax.all_gather(p_sum, 'tensor', axis=0, tiled=True)]
    dot_general x4 -> x0, matrix products: 18.6 us -> none  [the longest x1 5.95 us: local(): lax.dot_general(corrected, p_orth, contract_rows, precision=highest, pref...]
  transfers between devices with their start and end apart: 3 -> 0, of which waited for: 3 -> 0; matrix products, arithmetic and copies ran while one was open for 0% -> 0% of each run, Pallas kernels for 0% -> 0%
where the time goes in v1:
time: 103 us
  Pallas kernels  98.8 us (96%)
  local copies, waits for them, and re-layouts  3.74 us (4%)
    pallas_call x1, Pallas kernels, local(): pl.pallas_call(kernel, name='powersgd', out_shape=(jax.ShapeDtypeStruct((...  98.8 us
    unnamed x2, local copies, waits for them, and re-layouts  3.74 us

profile of v1, /device:TPU:1, one launch (start us, length us, event | category | flops | bytes accessed | tf_op | source)
XLA Modules:
  0.0 103.2 jit_solution(9888652574567546197)
XLA Ops:
  0.6 98.8 %powersgd.1 = (f32[64,256]{1,0:T(8,128)}, f32[64,4096]{1,0:T(8,128)}) custom-call(bf16[768,256]{1,0:T(8,128)(2,1)} %act_hbm.1, bf16[768,4096]{1,0:T(8,128)(2,1)} %grd_hbm.1, bf16[256,4096]{1,0:T(8,128)(2,1)} %bitcast.4, f32[64,4096]{1,0:T(8,128)} %bitcast.5), custom_call_target="tpu_custom_call" | custom-call | tf_op jit(solution)/shard_map/powersgd/pallas_call | solution.py:291
  99.5 1.5 %copy.8 = f32[256,64]{0,1:T(8,128)} copy(f32[256,64]{0,1:T(8,128)} %bitcast.7) | data formatting | bytes 131072
  100.9 2.3 %copy.9 = f32[4096,64]{0,1:T(8,128)} copy(f32[4096,64]{0,1:T(8,128)} %bitcast.6) | data formatting | bytes 2097152

commit v2 on v1

--- a/solution.py
+++ b/solution.py
@@ -13,9 +13,13 @@
 NT = 16
 RANK = 64
 LANES = 128
-WIN = 8
+WIN = 4
+ROWS = RANK // WIN
 GROUPS = NZ // WIN
+FAR_ORDER = sorted(range(1, GROUPS), key=lambda m: -min(m, GROUPS - m))
 LEFT, RIGHT = -(WIN // 2 - 1), WIN // 2
+ORDER = (10, 11, 14, 9, 6, 15, 5, 7, 13, 2, 8, 1, 4, 3, 12, 0)
+BATCH = 4
 NN = (((1,), (0,)), ((), ()))
 NT_DIMS = (((1,), (1,)), ((), ()))
 
@@ -59,12 +63,13 @@
            x, act, q0, q3, w3, p_src, p_rs, p_far, p_red, p_all,
            g_src, g_rs, g_own, g_all,
            q_loc, q_d, q_s, q_x, z_src, z_rs, z_far, z_red, z_all,
-           load_sem, send_sem, recv_sem, piece_sem):
+           load_sem, send_sem, recv_sem, piece_sem, relay_sem):
     dp = lax.axis_index("dp")
     t = lax.axis_index("tensor")
     z = dp // 2
     core = dp % 2
     other = 1 - core
+    sibling = (dp + other - core, t)
     place = z % WIN
     group = z // WIN
 
@@ -78,7 +83,7 @@
             device_id=dev, device_id_type=MESH).start()
 
     def tile(i):
-        return pl.ds(pl.multiple_of(i * 8, 8), 8)
+        return pl.ds(pl.multiple_of(i * ROWS, ROWS), ROWS)
 
     copies = [pltpu.make_async_copy(q0_hbm, q0, load_sem.at[0])]
     copies.append(pltpu.make_async_copy(err_hbm, x.at[pl.ds(768, 256)], load_sem.at[1]))
@@ -95,7 +100,8 @@
         cc = core if c == 0 else other
         if (d, c) != (0, 0):
             pl.semaphore_signal(barrier, inc=1, device_id=(at(z + d, cc), t), device_id_type=MESH)
-    for d in (-WIN, WIN):
+    far = [d for d in (-8, 8, -4, 4) if abs(d) > WIN // 2]
+    for d in far:
         pl.semaphore_signal(barrier, inc=1, device_id=(at(z + d, core), t), device_id_type=MESH)
     for k in range(1, NT):
         pl.semaphore_signal(barrier, inc=1, device_id=(dp, t ^ k), device_id_type=MESH)
@@ -112,7 +118,9 @@
         term = dot(split3(y), act[256 * r:256 * (r + 1), :])
         acc = term if acc is None else acc + term
     p_src[...] = fold3(acc) + left
-    pl.semaphore_wait(barrier, 2 * (WIN + 1) - 1 + 2 + NT - 1)
+    pl.semaphore_wait(barrier, len(near) - 1 + len(far) + NT - 1)
+    for d in (-8, 8):
+        pl.semaphore_signal(relay_sem, inc=1, device_id=(at(z + d, core), t), device_id_type=MESH)
 
     slot = 0
     for d in range(LEFT, RIGHT + 1):
@@ -131,14 +139,13 @@
     for s in range(2 * WIN - 1):
         total = total + p_rs[s]
     p_far[group] = total
-    send(p_far.at[group], p_far.at[group], 1, (at(z - WIN, core), t))
-    send(p_far.at[group], p_far.at[group], 1, (at(z + WIN, core), t))
-    wait(recv_sem.at[1], p_rs.at[pl.ds(0, 2)])
-    step = 1 - 2 * core
-    relay = (group + step + GROUPS) % GROUPS
-    send(p_far.at[relay], p_far.at[relay], 2, (at(z - step * WIN, core), t))
-    wait(recv_sem.at[2], p_rs.at[0])
-    total = (p_far[0] + p_far[1]) + (p_far[2] + p_far[3])
+    pl.semaphore_wait(relay_sem, 2)
+    for m in FAR_ORDER:
+        send(p_far.at[group], p_far.at[group], 1, (at(z + m * WIN, core), t))
+    wait(recv_sem.at[1], p_far.at[pl.ds(0, GROUPS - 1)])
+    total = p_far[0]
+    for m in range(1, GROUPS):
+        total = total + p_far[m]
     p_red[...] = total
     rows, cols = tile(place), pl.ds(pl.multiple_of(core * LANES, LANES), LANES)
     p_all[rows, cols] = total
@@ -150,37 +157,40 @@
     wait(recv_sem.at[3], p_rs)
 
     p_sum = p_all[...]
+
+    p3 = split3(p_sum)
+    w3[:, 768:1024] = p3
+    w3[:, 0:768] = split3(fold3(dot(p3, act[...], NT_DIMS)))
+
+    def compute(b):
+        for i in range(b * BATCH, (b + 1) * BATCH):
+            j = t ^ ORDER[i]
+            v = fold3(dot(w3[...], x[:, pl.ds(pl.multiple_of(j * 256, 256), 256)]))
+            q_loc[0, i] = v[:, :LANES]
+            q_loc[1, i] = v[:, LANES:]
+        part = pl.ds(b * BATCH, BATCH)
+        send(q_loc.at[other, part], q_d.at[part], 5, sibling, piece_sem.at[b])
+
+    def forward(b):
+        part = pl.ds(b * BATCH, BATCH)
+        wait(piece_sem.at[b], q_d.at[part])
+        q_s[part] = q_loc[core, part] + q_d[part]
+        for i in range(b * BATCH, min((b + 1) * BATCH, NT - 1)):
+            send(q_s.at[i], q_x.at[i], 6, (dp, t ^ ORDER[i]))
+
+    batches = NT // BATCH
+    for b in range(batches + 1):
+        if b < batches:
+            compute(b)
+        if b > 0:
+            forward(b - 1)
+
     gram = dot(p_sum, jnp.concatenate([p_sum, p_sum], axis=0), NT_DIMS, HIGHEST)
     for i in range(NT):
         g_src[i, 0:4, :] = gram[4 * i:4 * i + 4]
         g_src[i, 4:8, :] = gram[4 * i:4 * i + 4]
     for k in range(1, NT):
         send(g_src.at[t ^ k], g_rs.at[k - 1], 4, (dp, t ^ k))
-
-    p3 = split3(p_sum)
-    w3[:, 768:1024] = p3
-    w3[:, 0:768] = split3(fold3(dot(p3, act[...], NT_DIMS)))
-
-    def chunk(k):
-        j = t ^ k
-        v = fold3(dot(w3[...], x[:, pl.ds(pl.multiple_of(j * 256, 256), 256)]))
-        q_loc[k, 0] = v[:, :LANES]
-        q_loc[k, 1] = v[:, LANES:]
-        send(q_loc.at[k, other], q_d.at[k], 5, (dp + other - core, t), piece_sem.at[k])
-
-    def forward(k):
-        wait(piece_sem.at[k], q_d.at[k])
-        q_s[k] = q_loc[k, core] + q_d[k]
-        if k > 0:
-            send(q_s.at[k], q_x.at[k - 1], 6, (dp, t ^ k))
-
-    order = list(range(1, NT)) + [0]
-    lag = 6
-    for i in range(NT + lag):
-        if i < NT:
-            chunk(order[i])
-        if i >= lag:
-            forward(order[i - lag])
 
     wait(recv_sem.at[4], g_rs)
     total = g_src[t]
@@ -192,7 +202,7 @@
         send(g_own, g_all.at[t], 7, (dp, t ^ k))
 
     wait(recv_sem.at[6], q_x)
-    total = q_s[0]
+    total = q_s[NT - 1]
     for k in range(NT - 1):
         total = total + q_x[k]
     z_src[...] = total
@@ -209,15 +219,17 @@
     for s in range(WIN - 1):
         total = total + z_rs[s]
     z_far[group] = total
-    for m in range(1, GROUPS):
+    for m in FAR_ORDER:
         send(z_far.at[group], z_far.at[group], 9, (at(z + m * WIN, core), t))
 
     wait(recv_sem.at[7], g_rs)
     inverse = invert_factor(jnp.concatenate([g_all[i, 0:4, :] for i in range(NT)], axis=0))
     pb_ref[...] = dot(inverse, p_sum, NN, HIGHEST) * 64.0
 
-    wait(recv_sem.at[9], z_rs.at[pl.ds(0, GROUPS - 1)])
-    total = (z_far[0] + z_far[1]) + (z_far[2] + z_far[3])
+    wait(recv_sem.at[9], z_far.at[pl.ds(0, GROUPS - 1)])
+    total = z_far[0]
+    for m in range(1, GROUPS):
+        total = total + z_far[m]
     z_red[...] = total
     z_all[rows, :] = total
     for d in range(LEFT, RIGHT + 1):
@@ -230,29 +242,38 @@
 
     mine = columns(t, core)
     out_ref[:, mine] = dot(inverse, z_all[...], NN, HIGHEST) * (1.0 / 64.0)
-    for k in range(1, NT):
-        send(out_ref.at[:, mine], out_ref.at[:, mine], 11, (dp, t ^ k), piece_sem.at[NT + k])
-    sibling = (dp + other - core, t)
+    for i in range(NT - 1):
+        send(out_ref.at[:, mine], out_ref.at[:, mine], 11, (dp, t ^ ORDER[i]), piece_sem.at[NT + i])
     send(out_ref.at[:, mine], out_ref.at[:, mine], 12, sibling)
-    for k in range(1, NT):
-        got = columns(t ^ k, core)
-        wait(piece_sem.at[NT + k], out_ref.at[:, got])
+    for i in reversed(range(NT - 1)):
+        got = columns(t ^ ORDER[i], core)
+        wait(piece_sem.at[NT + i], out_ref.at[:, got])
         send(out_ref.at[:, got], out_ref.at[:, got], 12, sibling)
     wait(recv_sem.at[12], q_d)
 
     wait(send_sem.at[0], p_rs)
-    wait(send_sem.at[1], p_rs.at[pl.ds(0, 2)])
-    wait(send_sem.at[2], p_rs.at[0])
+    wait(send_sem.at[1], p_far.at[pl.ds(0, GROUPS - 1)])
     wait(send_sem.at[3], p_rs)
     wait(send_sem.at[4], g_rs)
     wait(send_sem.at[5], q_d)
     wait(send_sem.at[6], q_x)
     wait(send_sem.at[7], g_rs)
     wait(send_sem.at[8], z_rs)
-    wait(send_sem.at[9], z_rs.at[pl.ds(0, GROUPS - 1)])
+    wait(send_sem.at[9], z_far.at[pl.ds(0, GROUPS - 1)])
     wait(send_sem.at[10], z_rs)
     wait(send_sem.at[11], q_x)
     wait(send_sem.at[12], q_d)
+
+
+def store(basis, right, basis_hbm, right_hbm, sem):
+    copies = [pltpu.make_async_copy(basis, basis_hbm, sem.at[4])]
+    for i in range(4):
+        rows = pl.ds(i * 16, 16)
+        copies.append(pltpu.make_async_copy(right.at[rows], right_hbm.at[rows], sem.at[i]))
+    for c in copies:
+        c.start()
+    for c in copies:
+        c.wait()
 
 
 def local(activations, out_grads, error_memory, q_init):
@@ -266,41 +287,50 @@
         pltpu.VMEM((3 * RANK, 4096), BF16),
         pltpu.VMEM((3 * RANK, 1024), BF16),
         pltpu.VMEM((RANK, 256), F32),
-        pltpu.VMEM((2 * WIN - 1, 8, LANES), F32),
-        pltpu.VMEM((GROUPS, 8, LANES), F32),
-        pltpu.VMEM((8, LANES), F32),
+        pltpu.VMEM((2 * WIN - 1, ROWS, LANES), F32),
+        pltpu.VMEM((GROUPS, ROWS, LANES), F32),
+        pltpu.VMEM((ROWS, LANES), F32),
         pltpu.VMEM((RANK, 256), F32),
         pltpu.VMEM((NT, 8, LANES), F32),
         pltpu.VMEM((NT - 1, 8, LANES), F32),
         pltpu.VMEM((8, LANES), F32),
         pltpu.VMEM((NT, 8, LANES), F32),
-        pltpu.VMEM((NT, 2) + piece, F32),
+        pltpu.VMEM((2, NT) + piece, F32),
         pltpu.VMEM((NT,) + piece, F32),
         pltpu.VMEM((NT,) + piece, F32),
         pltpu.VMEM((NT - 1,) + piece, F32),
         pltpu.VMEM(piece, F32),
-        pltpu.VMEM((WIN - 1, 8, LANES), F32),
-        pltpu.VMEM((GROUPS, 8, LANES), F32),
-        pltpu.VMEM((8, LANES), F32),
+        pltpu.VMEM((WIN - 1, ROWS, LANES), F32),
+        pltpu.VMEM((GROUPS, ROWS, LANES), F32),
+        pltpu.VMEM((ROWS, LANES), F32),
         pltpu.VMEM(piece, F32),
         pltpu.SemaphoreType.DMA((6,)),
         pltpu.SemaphoreType.DMA((13,)),
         pltpu.SemaphoreType.DMA((13,)),
         pltpu.SemaphoreType.DMA((2 * NT,)),
+        pltpu.SemaphoreType.REGULAR,
     ]
     basis, right = pl.pallas_call(
         kernel,
         name="powersgd",
-        out_shape=(
-            jax.ShapeDtypeStruct((RANK, 256), F32),
-            jax.ShapeDtypeStruct((RANK, 4096), F32),
-        ),
+        out_shape=(pltpu.VMEM((RANK, 256), F32), pltpu.VMEM((RANK, 4096), F32)),
         in_specs=[any_spec] * 4,
         out_specs=(vmem, vmem),
         scratch_shapes=scratch,
         compiler_params=pltpu.CompilerParams(
             collective_id=0, has_side_effects=True, vmem_limit_bytes=60 * 2**20),
     )(activations, out_grads, error_memory[0], q_init.T)
+    basis, right = pl.pallas_call(
+        store,
+        name="store",
+        out_shape=(
+            jax.ShapeDtypeStruct((RANK, 256), F32),
+            jax.ShapeDtypeStruct((RANK, 4096), F32),
+        ),
+        in_specs=[vmem] * 2,
+        out_specs=(any_spec, any_spec),
+        scratch_shapes=[pltpu.SemaphoreType.DMA((5,))],
+    )(basis, right)
     return basis.T, right.T
 
 

time: 103 us -> 94.9 us (0.921)
  Pallas kernels: 98.8 us -> 92.5 us
  local copies, waits for them, and re-layouts: 3.74 us -> 1.57 us
    pallas_call x1 -> x2, Pallas kernels: 98.8 us -> 92.5 us  [the longest x1 90.2 us: local(): pl.pallas_call(kernel, name='powersgd', out_shape=(pltpu.VMEM((RANK, 256)...]
    unnamed x2 -> x4, local copies, waits for them, and re-layouts: 3.74 us -> 1.57 us
where the time goes in v2:
time: 94.9 us; the launch traced here: 94.7 us
  Pallas kernels  92.5 us (97%)
  local copies, waits for them, and re-layouts  1.57 us (2%)
    pallas_call x1, Pallas kernels, local(): pl.pallas_call(kernel, name='powersgd', out_shape=(pltpu.VMEM((RANK, 256)...  90.2 us
    pallas_call x1, Pallas kernels, local(): pl.pallas_call(store, name='store', out_shape=(jax.ShapeDtypeStruct((RANK...  2.29 us

profile of v2, /device:TPU:1, one launch (start us, length us, event | category | flops | bytes accessed | tf_op | source)
XLA Modules:
  0.0 94.7 jit_solution(1289321405431154939)
XLA Ops:
  0.6 90.2 %powersgd.1 = (f32[64,256]{1,0:T(8,128)S(1)}, f32[64,4096]{1,0:T(8,128)S(1)}) custom-call(bf16[768,256]{1,0:T(8,128)(2,1)} %act_hbm.1, bf16[768,4096]{1,0:T(8,128)(2,1)} %grd_hbm.1, bf16[256,4096]{1,0:T(8,128)(2,1)} %bitcast.4, f32[64,4096]{1,0:T(8,128)} %bitcast.5), custom_call_target="tpu_custom_call" | custom-call | tf_op jit(solution)/shard_map/powersgd/pallas_call | solution.py:313
  90.8 0.0 copy-start
  90.8 1.0 %copy-done = f32[64,4096]{1,0:T(8,128)} copy-done((f32[64,4096]{1,0:T(8,128)}, f32[64,4096]{1,0:T(8,128)S(1)}, u32[]{:S(2)}) %copy-start) | copy-done | bytes 1048600
  91.8 0.0 copy-start.1
  91.8 0.6 copy-done.1
  92.4 2.3 %store.1 = (f32[64,256]{1,0:T(8,128)}, f32[64,4096]{1,0:T(8,128)}) custom-call(f32[64,256]{1,0:T(8,128)} %copy-done.1, f32[64,4096]{1,0:T(8,128)} %copy-done), custom_call_target="tpu_custom_call" | custom-call | tf_op jit(solution)/shard_map/store/pallas_call | solution.py:323
Async XLA Ops:
  90.8 1.0 %copy-start = (f32[64,4096]{1,0:T(8,128)}, f32[64,4096]{1,0:T(8,128)S(1)}, u32[]{:S(2)}) copy-start(f32[64,4096]{1,0:T(8,128)S(1)} %get-tuple-element.7.right) | copy-start | bytes 3145732
  91.8 0.6 copy-start.1

commit v3 on v2

--- a/solution.py
+++ b/solution.py
@@ -17,7 +17,7 @@
 ROWS = RANK // WIN
 GROUPS = NZ // WIN
 FAR_ORDER = sorted(range(1, GROUPS), key=lambda m: -min(m, GROUPS - m))
-LEFT, RIGHT = -(WIN // 2 - 1), WIN // 2
+WINDOW = sorted(range(-(WIN // 2 - 1), WIN // 2 + 1), key=lambda d: -abs(d))
 ORDER = (10, 11, 14, 9, 6, 15, 5, 7, 13, 2, 8, 1, 4, 3, 12, 0)
 BATCH = 4
 NN = (((1,), (0,)), ((), ()))
@@ -100,8 +100,7 @@
         cc = core if c == 0 else other
         if (d, c) != (0, 0):
             pl.semaphore_signal(barrier, inc=1, device_id=(at(z + d, cc), t), device_id_type=MESH)
-    far = [d for d in (-8, 8, -4, 4) if abs(d) > WIN // 2]
-    for d in far:
+    for d in (-WIN, WIN, -8, 8):
         pl.semaphore_signal(barrier, inc=1, device_id=(at(z + d, core), t), device_id_type=MESH)
     for k in range(1, NT):
         pl.semaphore_signal(barrier, inc=1, device_id=(dp, t ^ k), device_id_type=MESH)
@@ -118,12 +117,12 @@
         term = dot(split3(y), act[256 * r:256 * (r + 1), :])
         acc = term if acc is None else acc + term
     p_src[...] = fold3(acc) + left
-    pl.semaphore_wait(barrier, len(near) - 1 + len(far) + NT - 1)
+    pl.semaphore_wait(barrier, len(near) - 1 + 4 + NT - 1)
     for d in (-8, 8):
         pl.semaphore_signal(relay_sem, inc=1, device_id=(at(z + d, core), t), device_id_type=MESH)
 
     slot = 0
-    for d in range(LEFT, RIGHT + 1):
+    for d in WINDOW:
         e = -d
         for same in (0, 1):
             if d == 0 and same == 1:
@@ -149,7 +148,7 @@
     p_red[...] = total
     rows, cols = tile(place), pl.ds(pl.multiple_of(core * LANES, LANES), LANES)
     p_all[rows, cols] = total
-    for d in range(LEFT, RIGHT + 1):
+    for d in WINDOW:
         for same in (0, 1):
             if d == 0 and same == 1:
                 continue
@@ -178,19 +177,22 @@
         for i in range(b * BATCH, min((b + 1) * BATCH, NT - 1)):
             send(q_s.at[i], q_x.at[i], 6, (dp, t ^ ORDER[i]))
 
+    def gram_tiles():
+        gram = dot(p_sum, jnp.concatenate([p_sum, p_sum], axis=0), NT_DIMS, HIGHEST)
+        for i in range(NT):
+            g_src[i, 0:4, :] = gram[4 * i:4 * i + 4]
+            g_src[i, 4:8, :] = gram[4 * i:4 * i + 4]
+        for k in range(1, NT):
+            send(g_src.at[t ^ k], g_rs.at[k - 1], 4, (dp, t ^ k))
+
     batches = NT // BATCH
     for b in range(batches + 1):
         if b < batches:
             compute(b)
         if b > 0:
             forward(b - 1)
-
-    gram = dot(p_sum, jnp.concatenate([p_sum, p_sum], axis=0), NT_DIMS, HIGHEST)
-    for i in range(NT):
-        g_src[i, 0:4, :] = gram[4 * i:4 * i + 4]
-        g_src[i, 4:8, :] = gram[4 * i:4 * i + 4]
-    for k in range(1, NT):
-        send(g_src.at[t ^ k], g_rs.at[k - 1], 4, (dp, t ^ k))
+        if b == 2:
+            gram_tiles()
 
     wait(recv_sem.at[4], g_rs)
     total = g_src[t]
@@ -208,7 +210,7 @@
     z_src[...] = total
 
     slot = 0
-    for d in range(LEFT, RIGHT + 1):
+    for d in WINDOW:
         if d != 0:
             piece = (z - d + NZ) % WIN
             send(z_src.at[tile(piece)], z_rs.at[slot], 8, (at(z - d, core), t))
@@ -232,7 +234,7 @@
         total = total + z_far[m]
     z_red[...] = total
     z_all[rows, :] = total
-    for d in range(LEFT, RIGHT + 1):
+    for d in WINDOW:
         if d != 0:
             send(z_red, z_all.at[rows], 10, (at(z + d, core), t))
     wait(recv_sem.at[10], z_rs)
@@ -245,7 +247,7 @@
     for i in range(NT - 1):
         send(out_ref.at[:, mine], out_ref.at[:, mine], 11, (dp, t ^ ORDER[i]), piece_sem.at[NT + i])
     send(out_ref.at[:, mine], out_ref.at[:, mine], 12, sibling)
-    for i in reversed(range(NT - 1)):
+    for i in range(NT - 1):
         got = columns(t ^ ORDER[i], core)
         wait(piece_sem.at[NT + i], out_ref.at[:, got])
         send(out_ref.at[:, got], out_ref.at[:, got], 12, sibling)
@@ -305,8 +307,8 @@
         pltpu.VMEM((ROWS, LANES), F32),
         pltpu.VMEM(piece, F32),
         pltpu.SemaphoreType.DMA((6,)),
-        pltpu.SemaphoreType.DMA((13,)),
-        pltpu.SemaphoreType.DMA((13,)),
+        pltpu.SemaphoreType.DMA((14,)),
+        pltpu.SemaphoreType.DMA((14,)),
         pltpu.SemaphoreType.DMA((2 * NT,)),
         pltpu.SemaphoreType.REGULAR,
     ]
@@ -327,9 +329,10 @@
             jax.ShapeDtypeStruct((RANK, 256), F32),
             jax.ShapeDtypeStruct((RANK, 4096), F32),
         ),
-        in_specs=[vmem] * 2,
+        in_specs=[any_spec] * 2,
         out_specs=(any_spec, any_spec),
         scratch_shapes=[pltpu.SemaphoreType.DMA((5,))],
+        compiler_params=pltpu.CompilerParams(vmem_limit_bytes=2**20),
     )(basis, right)
     return basis.T, right.T
 

time: 94.9 us -> 91 us (0.959)
  Pallas kernels: 92.5 us -> 90.2 us
  local copies, waits for them, and re-layouts: 1.57 us -> 0 us
    unnamed x4 -> x0, local copies, waits for them, and re-layouts: 1.57 us -> none
    pallas_call x1, Pallas kernels: 2.29 us -> 1.03 us  [local(): pl.pallas_call(store, name='store', out_shape=(jax.ShapeDtypeStruct((RANK...]
    pallas_call x1, Pallas kernels: 90.2 us -> 89.2 us  [local(): pl.pallas_call(kernel, name='powersgd', out_shape=(pltpu.VMEM((RANK, 256)...]
where the time goes in v3:
time: 91 us; the launch traced here: 90.8 us
  Pallas kernels  90.2 us (99%)
    pallas_call x1, Pallas kernels, local(): pl.pallas_call(kernel, name='powersgd', out_shape=(pltpu.VMEM((RANK, 256)...  89.2 us

profile of v3, /device:TPU:1, one launch (start us, length us, event | category | flops | bytes accessed | tf_op | source)
XLA Modules:
  0.0 90.8 jit_solution(16499439459161106438)
XLA Ops:
  0.6 89.2 %powersgd.1 = (f32[64,256]{1,0:T(8,128)S(1)}, f32[64,4096]{1,0:T(8,128)S(1)}) custom-call(bf16[768,256]{1,0:T(8,128)(2,1)} %act_hbm.1, bf16[768,4096]{1,0:T(8,128)(2,1)} %grd_hbm.1, bf16[256,4096]{1,0:T(8,128)(2,1)} %bitcast.4, f32[64,4096]{1,0:T(8,128)} %bitcast.5), custom_call_target="tpu_custom_call" | custom-call | tf_op jit(solution)/shard_map/powersgd/pallas_call | solution.py:315
  89.8 1.0 %store.1 = (f32[64,256]{1,0:T(8,128)}, f32[64,4096]{1,0:T(8,128)}) custom-call(f32[64,256]{1,0:T(8,128)S(1)} %get-tuple-element.6.basis, f32[64,4096]{1,0:T(8,128)S(1)} %get-tuple-element.7.right), custom_call_target="tpu_custom_call" | custom-call | tf_op jit(solution)/shard_map/store/pallas_call | solution.py:325

commit v4 on v3

--- a/solution.py
+++ b/solution.py
@@ -28,16 +28,13 @@
     return lax.dot_general(a, b, dims, precision=precision, preferred_element_type=F32)
 
 
-def split3(v):
-    hi = v.astype(BF16)
-    rest = v - hi.astype(F32)
-    mid = rest.astype(BF16)
-    low = (rest - mid.astype(F32)).astype(BF16)
-    return jnp.concatenate([hi, mid, low], axis=0)
-
-
-def fold3(v):
-    return v[:RANK] + (v[RANK:2 * RANK] + v[2 * RANK:])
+def split(v):
+    high = v.astype(BF16)
+    return jnp.concatenate([high, (v - high.astype(F32)).astype(BF16)], axis=0)
+
+
+def fold(v):
+    return v[:RANK] + v[RANK:]
 
 
 def wait(sem, ref):
@@ -60,7 +57,7 @@
 
 
 def kernel(act_hbm, grd_hbm, err_hbm, q0_hbm, pb_ref, out_ref,
-           x, act, q0, q3, w3, p_src, p_rs, p_far, p_red, p_all,
+           x, act, q0, q2, w2, p_src, p_rs, p_far, p_red, p_all,
            g_src, g_rs, g_own, g_all,
            q_loc, q_d, q_s, q_x, z_src, z_rs, z_far, z_red, z_all,
            load_sem, send_sem, recv_sem, piece_sem, relay_sem):
@@ -91,8 +88,8 @@
         copies.append(pltpu.make_async_copy(
             grd_hbm.at[pl.ds(256 * r, 256)], x.at[pl.ds(256 * r, 256)], load_sem.at[2 + r]))
     copies.append(pltpu.make_async_copy(act_hbm, act, load_sem.at[5]))
-    for c in copies:
-        c.start()
+    for i in (0, 1, 5, 2, 3, 4):
+        copies[i].start()
 
     barrier = pltpu.get_barrier_semaphore()
     near = [(d, c) for d in range(-WIN // 2, WIN // 2 + 1) for c in (0, 1)]
@@ -106,17 +103,17 @@
         pl.semaphore_signal(barrier, inc=1, device_id=(dp, t ^ k), device_id_type=MESH)
 
     copies[0].wait()
-    q3[...] = split3(q0[...])
+    q2[...] = split(q0[...])
     copies[1].wait()
-    left = fold3(dot(q3[...], x[768:1024, :], NT_DIMS))
+    left = fold(dot(q2[...], x[768:1024, :], NT_DIMS))
     copies[5].wait()
     acc = None
     for r in range(3):
         copies[2 + r].wait()
-        y = fold3(dot(q3[...], x[256 * r:256 * (r + 1), :], NT_DIMS))
-        term = dot(split3(y), act[256 * r:256 * (r + 1), :])
+        y = fold(dot(q2[...], x[256 * r:256 * (r + 1), :], NT_DIMS))
+        term = dot(split(y), act[256 * r:256 * (r + 1), :])
         acc = term if acc is None else acc + term
-    p_src[...] = fold3(acc) + left
+    p_src[...] = fold(acc) + left
     pl.semaphore_wait(barrier, len(near) - 1 + 4 + NT - 1)
     for d in (-8, 8):
         pl.semaphore_signal(relay_sem, inc=1, device_id=(at(z + d, core), t), device_id_type=MESH)
@@ -157,14 +154,14 @@
 
     p_sum = p_all[...]
 
-    p3 = split3(p_sum)
-    w3[:, 768:1024] = p3
-    w3[:, 0:768] = split3(fold3(dot(p3, act[...], NT_DIMS)))
+    p2 = split(p_sum)
+    w2[:, 768:1024] = p2
+    w2[:, 0:768] = split(fold(dot(p2, act[...], NT_DIMS)))
 
     def compute(b):
         for i in range(b * BATCH, (b + 1) * BATCH):
             j = t ^ ORDER[i]
-            v = fold3(dot(w3[...], x[:, pl.ds(pl.multiple_of(j * 256, 256), 256)]))
+            v = fold(dot(w2[...], x[:, pl.ds(pl.multiple_of(j * 256, 256), 256)]))
             q_loc[0, i] = v[:, :LANES]
             q_loc[1, i] = v[:, LANES:]
         part = pl.ds(b * BATCH, BATCH)
@@ -286,8 +283,8 @@
         pltpu.VMEM((1024, 4096), BF16),
         pltpu.VMEM((768, 256), BF16),
         pltpu.VMEM((RANK, 4096), F32),
-        pltpu.VMEM((3 * RANK, 4096), BF16),
-        pltpu.VMEM((3 * RANK, 1024), BF16),
+        pltpu.VMEM((2 * RANK, 4096), BF16),
+        pltpu.VMEM((2 * RANK, 1024), BF16),
         pltpu.VMEM((RANK, 256), F32),
         pltpu.VMEM((2 * WIN - 1, ROWS, LANES), F32),
         pltpu.VMEM((GROUPS, ROWS, LANES), F32),

time: 91 us -> 90.1 us (level)
  no operation moved by 1% of the time
where the time goes in v4:
time: 90.1 us; the launch traced here: 89.9 us
  Pallas kernels  89.3 us (99%)
    pallas_call x1, Pallas kernels, local(): pl.pallas_call(kernel, name='powersgd', out_shape=(pltpu.VMEM((RANK, 256)...  88.3 us

profile of v4, /device:TPU:1, one launch (start us, length us, event | category | flops | bytes accessed | tf_op | source)
XLA Modules:
  0.0 89.9 jit_solution(13508307954878099480)
XLA Ops:
  0.6 88.3 %powersgd.1 = (f32[64,256]{1,0:T(8,128)S(1)}, f32[64,4096]{1,0:T(8,128)S(1)}) custom-call(bf16[768,256]{1,0:T(8,128)(2,1)} %act_hbm.1, bf16[768,4096]{1,0:T(8,128)(2,1)} %grd_hbm.1, bf16[256,4096]{1,0:T(8,128)(2,1)} %bitcast.4, f32[64,4096]{1,0:T(8,128)} %bitcast.5), custom_call_target="tpu_custom_call" | custom-call | tf_op jit(solution)/shard_map/powersgd/pallas_call | solution.py:312
  88.9 1.0 %store.1 = (f32[64,256]{1,0:T(8,128)}, f32[64,4096]{1,0:T(8,128)}) custom-call(f32[64,256]{1,0:T(8,128)S(1)} %get-tuple-element.6.basis, f32[64,4096]{1,0:T(8,128)S(1)} %get-tuple-element.7.right), custom_call_target="tpu_custom_call" | custom-call | tf_op jit(solution)/shard_map/store/pallas_call | solution.py:322
